TPU v7x, 32 devices: a whole 2x2x4 slice. The times are simulated.
32 devices in a mesh: groups: 1, row: 8 (over z, y), col: 4 (over x, core).
Axes of the slice: x: 2, y: 2, z: 4, core: 2. Of those that a mesh axis runs over, the one named last changes fastest.
Arguments:
- activations: bfloat16 [1024, 16384], P('groups', ('row', 'col')), may hold values from -2.5 to 2.5
- token_ids: int32 [1024], P('groups'), may hold values from 0 to 128255
- initial: float32 [16384, 256], P(('groups', 'row', 'col')), may hold values from -6 to 6
- block_mask: int32 [128, 2], P('groups'), may hold values 0 or 1
Outputs:
- gram: float32 [8, 4, 512, 16384], P('groups', 'col', None, 'row')
- repaired: float32 [16384, 256], P(('groups', 'row', 'col'))
All inputs are finite; a program needn't handle non-finite values.
Results may differ from a plain program's by a relative error of at most 0.0003.
Values may be sent and summed in bfloat16 or wider, within the bound.
A program may use at most 128 MiB of HBM per device.

v0:
```python
import math

import jax
import jax.numpy as jnp
from jax import lax
from jax.sharding import PartitionSpec as P

D = 16384
ROWS = 1024
BLOCK = 128
ITERS = 2


def shards(activations, token_ids, initial, block_mask):
    matches = (token_ids[:, None] == token_ids[None, :]).astype(jnp.float32)
    weights = 1.0 / jnp.sum(matches, axis=1)
    weighted = (activations.astype(jnp.float32) * weights[:, None]).astype(jnp.bfloat16)
    column_panel = lax.all_gather(activations, "col", axis=1, tiled=True)
    gram_tile = lax.dot_general(
        lax.all_gather(weighted, "row", axis=1, tiled=True),
        column_panel,
        (((0,), (0,)), ((), ())),
        preferred_element_type=jnp.float32,
    ) * (1.0 / ROWS)
    shard_rows = initial.shape[0]
    col_count = lax.axis_size("col")
    first_feature = (lax.axis_index("row") * col_count + lax.axis_index("col")) * shard_rows
    block_index = (first_feature + jnp.arange(shard_rows, dtype=jnp.int32)) // BLOCK
    selector = (
        block_index[:, None] == jnp.arange(block_mask.shape[0], dtype=jnp.int32)[None, :]
    ).astype(jnp.float32)
    mask_rows = jnp.dot(selector, block_mask.astype(jnp.float32), precision=lax.Precision.HIGHEST)
    mask_full = jnp.repeat(mask_rows, BLOCK, axis=1)
    step_size = ROWS / (D + 2.0 * math.sqrt(D * ROWS) + ROWS)
    current = mask_full * initial
    for iteration in range(ITERS):
        change_now = current - initial
        projected = jnp.dot(
            activations.astype(jnp.float32), change_now, precision=lax.Precision.HIGHEST
        )
        totals = lax.psum(projected, ("row", "col"))
        pulled = lax.dot_general(
            weighted.astype(jnp.float32),
            totals,
            (((0,), (0,)), ((), ())),
            precision=lax.Precision.HIGHEST,
        ) * (1.0 / ROWS)
        current = mask_full * (current - step_size * pulled)
    gram_out = gram_tile.reshape(lax.axis_size("row"), 1, shard_rows, gram_tile.shape[1])
    return (gram_out, current)


def solution(mesh):
    in_specs = (
        P("groups", ("row", "col")),
        P("groups"),
        P(("groups", "row", "col"), None),
        P("groups", None),
    )
    out_specs = (P("groups", "col", None, "row"), P(("groups", "row", "col"), None))
    return jax.shard_map(shards, mesh=mesh, in_specs=in_specs, out_specs=out_specs, check_vma=False)
```

profile of v0, /device:TPU:1, one launch (start us, length us, event | category | flops | bytes accessed | tf_op | source)
XLA Modules:
  0.0 424.5 jit_solution(2539099986985370560)
XLA Ops:
  8.0 0.0 copy-start
  8.0 0.0 copy-start.2
  8.0 0.0 all-reduce.3.cloned.1.call-start
  8.1 1.1 fusion.8
  9.2 0.6 broadcast_in_dim.2
  9.8 4.3 %convolution_bitcast_fusion.1 = f32[1024,256]{0,1:T(8,128)} fusion(bf16[1024,512]{1,0:T(8,128)(2,1)} %param.4, f32[512,256]{1,0:T(8,128)} %param.6, f32[64,8,2,128]{3,2,1,0:T(2,128)S(1)} %bitcast.25), kind=kOutput, calls=%fused_computation.4 | convolution fusion | flops 1610874880 | bytes 3145728 | tf_op jit(solution)/shard_map/dot_general | solution.py:38
  14.1 0.0 all-reduce.3.cloned.1.call-update
  14.1 0.0 all-reduce.5.cloned.1.call-start
  14.1 0.0 copy-done.2
  14.1 0.5 convert_reduce_fusion
  14.7 0.0 copy-done
  14.7 0.3 multiply_convert_fusion
  15.0 0.0 copy-start.1
  15.0 130.2 %all-reduce.3.cloned.1.call-done = f32[1024,256]{0,1:T(8,128)} async-done(((f32[1024,256]{0,1:T(8,128)}), f32[1024,256]{0,1:T(8,128)}) %all-reduce.3.cloned.1.call-update) | async-done | bytes 1048592 | tf_op jit(solution)/shard_map/psum | solution.py:41
  145.3 2.6 fusion.1
  147.9 3.9 convolution_bitcast_fusion
  151.8 0.0 all-reduce.5.cloned.1.call-update
  151.8 0.0 all-gather.5.cloned.1.call-start
  151.9 0.5 all-gather.5.cloned.1.call-update
  152.4 0.0 copy-done.1
  152.4 0.2 all-gather.3.cloned.1.call-start
  152.6 0.4 all-gather.3.cloned.1.call-update
  153.0 234.6 %all-reduce.5.cloned.1.call-done = f32[1024,256]{0,1:T(8,128)} async-done(((f32[1024,256]{0,1:T(8,128)}), f32[1024,256]{0,1:T(8,128)}) %all-reduce.5.cloned.1.call-update) | async-done | bytes 1048592 | tf_op jit(solution)/shard_map/psum | solution.py:41
  387.6 3.6 fusion.3
  391.2 0.0 all-gather.5.cloned.1.call-done
  391.2 0.0 all-gather.3.cloned.1.call-done
  391.2 25.8 %convolution_multiply_fusion = f32[4096,2048]{1,0:T(8,128)} fusion(bf16[1024,4096]{1,0:T(8,128)(2,1)} %all-gather.3.cloned.1.call-done, bf16[1024,2048]{1,0:T(8,128)(2,1)} %all-gather.5.cloned.1.call-done), kind=kOutput, calls=%fused_computation | convolution fusion | flops 17188257792 | bytes 46137344 | tf_op jit(solution)/shard_map/dot_general | solution.py:19
  (2 shorter events, 0.0 us)
Async XLA Ops:
  8.0 6.7 %copy-start = (bf16[1024,512]{1,0:T(8,128)(2,1)S(1)}, bf16[1024,512]{1,0:T(8,128)(2,1)}, u32[]{:S(2)}) copy-start(bf16[1024,512]{1,0:T(8,128)(2,1)} %param.4) | copy-start | bytes 3145732
  8.0 6.1 %copy-start.2 = (s32[1024]{0:T(1024)S(1)}, s32[1024]{0:T(1024)}, u32[]{:S(2)}) copy-start(s32[1024]{0:T(1024)} %param.5) | copy-start | bytes 12292
  8.0 137.2 %all-reduce.3.cloned.1.call-start = ((), (), s32[]{:S(2)}) async-start(), calls=%async_computation.2 | async-start | bytes 2097152 | tf_op jit(solution)/shard_map/psum | solution.py:41
  14.1 373.5 %all-reduce.5.cloned.1.call-start = ((), (), s32[]{:S(2)}) async-start(), calls=%async_computation.3 | async-start | bytes 2097152 | tf_op jit(solution)/shard_map/psum | solution.py:41
  15.0 137.4 %copy-start.1 = (bf16[1024,512]{1,0:T(8,128)(2,1)}, bf16[1024,512]{1,0:T(8,128)(2,1)S(1)}, u32[]{:S(2)}) copy-start(bf16[1024,512]{1,0:T(8,128)(2,1)S(1)} %multiply_convert_fusion) | copy-start | bytes 3145732
  151.8 239.4 %all-gather.5.cloned.1.call-start = ((), (), s32[]{:S(2)}) async-start(), calls=%async_computation.1 | async-start | bytes 5242880 | tf_op jit(solution)/shard_map/all_gather | solution.py:18
  152.4 238.8 %all-gather.3.cloned.1.call-start = ((), (), s32[]{:S(2)}) async-start(), calls=%async_computation | async-start | bytes 9437184 | tf_op jit(solution)/shard_map/all_gather | solution.py:20
Sparse Core Ops, SparseCore 0:
  14.2 131.0 all-reduce.2
  151.9 235.6 all-reduce.4
Sparse Core Ops, SparseCore 1:
  153.8 35.1 all-gather.4
  191.4 124.5 all-gather.2
where the time goes:
time: 426 us; the launch traced here: 424 us
  waiting for transfers between devices  366 us (86%)
  matrix products  41.3 us (10%)
  between operations  15.6 us (4%)
    psum x2, waiting for transfers between devices, shards(): totals = lax.psum(projected, ('row', 'col'))  365 us
    dot_general x1, matrix products, shards(): lax.dot_general(lax.all_gather(weighted, 'row', axis=1, tiled=True), colu...  25.8 us
  transfers between devices with their start and end apart: 4, of which 2 were waited for; matrix products, arithmetic and copies ran while one was open for 1% of the time, Pallas kernels for 0%

commit v1 on v0

v1 whole, which is shorter than its diff:
```python
import functools
import math

import jax
import jax.numpy as jnp
from jax import lax
from jax.experimental import pallas as pl
from jax.experimental.pallas import tpu as pltpu
from jax.sharding import PartitionSpec as P

BLOCK = 128
ITERS = 2
PIECES = 2
VMEM_LIMIT = 48 * 1024 * 1024


def split_two(value):
    high = value.astype(jnp.bfloat16)
    return high, (value - high.astype(jnp.float32)).astype(jnp.bfloat16)


def exchange_kernel(
    n_row, n_col, step_size,
    wt_hbm, act_hbm, wt, act, init, mask,
    wt_all, act_all, cur,
    partial, from_col, part, from_row, tot, change2, tot2,
    gs, gr, xs, xr, own_sem, s1, r1, s2, r2, s3, r3, s4, r4,
):
    rows = act.shape[0]
    feats, outc = init.shape
    r, c = lax.axis_index("row"), lax.axis_index("col")
    z, y = r // 2, r % 2
    nz = n_row // 2
    x, core = c // 2, c % 2
    nx = n_col // 2
    up, down, side = r + 2, r - 2, z * 2 + (1 - y)
    sibling = x * 2 + (1 - core)
    row_peers = [lax.rem(r + k, n_row) for k in range(1, n_row)]
    col_peers = [lax.rem(c + k, n_col) for k in range(1, n_col)]

    barrier = pltpu.get_barrier_semaphore()
    for p in row_peers:
        pl.semaphore_signal(barrier, inc=1, device_id={"row": p}, device_id_type=pl.DeviceIdType.MESH)
    for p in col_peers:
        pl.semaphore_signal(barrier, inc=1, device_id={"col": p}, device_id_type=pl.DeviceIdType.MESH)
    pl.semaphore_wait(barrier, n_row + n_col - 2)

    def send(src, dst, ss, rs, where):
        return pltpu.make_async_remote_copy(
            src_ref=src, dst_ref=dst, send_sem=ss, recv_sem=rs,
            device_id=where, device_id_type=pl.DeviceIdType.MESH)

    def gcopy(a, h, way, peer, own=False):
        src = wt_hbm.at[h] if own else wt_all.at[a, h]
        return send(src, wt_all.at[a, h], gs.at[way, a, h], gr.at[a, h], {"row": peer})

    def own_pieces(act_on):
        for h in range(PIECES):
            @pl.when(z + 1 < nz)
            def _():
                act_on(gcopy(r, h, 0, up, True))

            @pl.when(z > 0)
            def _():
                act_on(gcopy(r, h, 1, down, True))

            act_on(gcopy(r, h, 2, side, True))

    def hop(d, h, act_on, arrive):
        @pl.when(z >= d)
        def _():
            a = r - 2 * d
            if arrive:
                gcopy(a, h, 2, side).wait_recv()

            @pl.when(z + 1 < nz)
            def _():
                act_on(gcopy(a, h, 0, up))

            act_on(gcopy(a, h, 2, side))

        @pl.when(z + d < nz)
        def _():
            a = r + 2 * d
            if arrive:
                gcopy(a, h, 2, side).wait_recv()

            @pl.when(z > 0)
            def _():
                act_on(gcopy(a, h, 1, down))

            act_on(gcopy(a, h, 2, side))

    start = lambda copy: copy.start()
    wait_send = lambda copy: copy.wait_send()

    hops = [(d, h) for d in range(1, nz) for h in range(PIECES)]
    hops_done = [0]

    def next_hop():
        if hops_done[0] < len(hops):
            d, h = hops[hops_done[0]]
            hop(d, h, start, True)
            hops_done[0] += 1

    def x_copies():
        copies = []
        for k in range(1, nx):
            p = lax.rem(x + k, nx) * 2 + core
            copies.append(send(act_hbm, act_all.at[c], xs.at[k], xr.at[c], {"col": p}))
        copies.append(send(act_hbm, act_all.at[c], xs.at[0], xr.at[c], {"col": sibling}))
        return copies

    def x_passed(k):
        a = lax.rem(x + k, nx) * 2 + core
        return send(act_all.at[a], act_all.at[a], xs.at[nx + k], xr.at[a], {"col": sibling})

    own_wt = pltpu.make_async_copy(wt_hbm, wt_all.at[r], own_sem.at[0])
    own_act = pltpu.make_async_copy(act_hbm, act_all.at[c], own_sem.at[1])
    own_pieces(start)

    chunk = rows // n_col
    cur[...] = mask[...] * init[...]
    pending = []

    for it in range(ITERS):
        high, low = split_two(cur[...] - init[...])
        change2[:, 0:outc] = high
        change2[:, outc:2 * outc] = low

        def project(j, carry):
            a = act[pl.ds(pl.multiple_of(j * chunk, chunk), chunk), :]
            both = jnp.dot(a, change2[...], preferred_element_type=jnp.float32)
            total = both[:, 0:outc] + both[:, outc:2 * outc]
            partial[it, j] = total.reshape(partial.shape[2:])
            return carry

        lax.fori_loop(0, n_col, project, 0)

        def exchange(copies):
            for copy in copies:
                copy.start()
            pending.extend(copies)

        exchange([send(partial.at[it, p], from_col.at[it, c], s1.at[it, k], r1.at[it, c], {"col": p})
                  for k, p in enumerate(col_peers)])
        if it == 0:
            own_wt.start()
            own_act.start()
        next_hop()
        for k, p in enumerate(col_peers):
            send(partial.at[it, p], from_col.at[it, p], s1.at[it, k], r1.at[it, p], {"col": p}).wait_recv()
        acc = partial[it, c]
        for p in col_peers:
            acc = acc + from_col[it, p]
        part[it] = acc
        exchange([send(part.at[it, p], from_row.at[it, r], s2.at[it, k], r2.at[it, r], {"row": p})
                  for k, p in enumerate(row_peers)])
        if it == 0:
            for copy in x_copies():
                copy.start()
        next_hop()
        for k, p in enumerate(row_peers):
            send(part.at[it, p], from_row.at[it, p], s2.at[it, k], r2.at[it, p], {"row": p}).wait_recv()
        acc = part[it, r]
        for p in row_peers:
            acc = acc + from_row[it, p]
        tot[it, c, r] = acc
        exchange([send(tot.at[it, c, r], tot.at[it, c, r], s3.at[it, k], r3.at[it, r], {"row": p})
                  for k, p in enumerate(row_peers)])
        if it > 0:
            next_hop()
        for k, p in enumerate(row_peers):
            send(tot.at[it, c, p], tot.at[it, c, p], s3.at[it, k], r3.at[it, p], {"row": p}).wait_recv()
        exchange([send(tot.at[it, c], tot.at[it, c], s4.at[it, k], r4.at[it, c], {"col": p})
                  for k, p in enumerate(col_peers)])
        next_hop()
        if it == 0:
            for k in range(1, nx):
                a = lax.rem(x + k, nx) * 2 + core
                x_passed(k).wait_recv()
                x_passed(k).start()
        for k, p in enumerate(col_peers):
            send(tot.at[it, p], tot.at[it, p], s4.at[it, k], r4.at[it, p], {"col": p}).wait_recv()

        high, low = split_two(tot[it].reshape(rows, outc))
        tot2[:, 0:outc] = high
        tot2[:, outc:2 * outc] = low

        def pull(j, carry):
            at = pl.ds(pl.multiple_of(j * BLOCK, BLOCK), BLOCK)
            both = jnp.dot(wt[at, :], tot2[...], preferred_element_type=jnp.float32)
            pulled = (both[:, 0:outc] + both[:, outc:2 * outc]) * (1.0 / rows)
            cur[at, :] = mask[at, :] * (cur[at, :] - step_size * pulled)
            return carry

        lax.fori_loop(0, feats // BLOCK, pull, 0)

    while hops_done[0] < len(hops):
        next_hop()
    for zz in range(nz):
        for h in range(PIECES):
            gcopy(zz * 2 + (1 - y), h, 2, side).wait_recv()
    for k in range(nx):
        a = lax.rem(x + k, nx) * 2 + (1 - core)
        send(act_all.at[a], act_all.at[a], xs.at[0], xr.at[a], {"col": sibling}).wait_recv()
    own_pieces(wait_send)
    for d, h in hops:
        hop(d, h, wait_send, False)
    for copy in x_copies():
        copy.wait_send()
    for k in range(1, nx):
        x_passed(k).wait_send()
    for copy in pending:
        copy.wait_send()
    own_wt.wait()
    own_act.wait()


def gram_kernel(scale, wt, act, out):
    feats = act.shape[2]
    for j in range(act.shape[0]):
        tile = jnp.dot(wt[0], act[j], preferred_element_type=jnp.float32) * scale
        out[0, 0, :, j * feats:(j + 1) * feats] = tile


def expanded_mask(block_mask, shard_rows, col_count):
    first_feature = (lax.axis_index("row") * col_count + lax.axis_index("col")) * shard_rows
    block_index = (first_feature + jnp.arange(shard_rows, dtype=jnp.int32)) // BLOCK
    selector = (
        block_index[:, None] == jnp.arange(block_mask.shape[0], dtype=jnp.int32)[None, :]
    ).astype(jnp.float32)
    mask_rows = jnp.dot(selector, block_mask.astype(jnp.float32), precision=lax.Precision.HIGHEST)
    return jnp.repeat(mask_rows, BLOCK, axis=1)


def weigh(activations, token_ids):
    matches = (token_ids[:, None] == token_ids[None, :]).astype(jnp.float32)
    weights = 1.0 / jnp.sum(matches, axis=1)
    return (activations.astype(jnp.float32) * weights[:, None]).astype(jnp.bfloat16)


def kernel_shards(n_row, n_col, activations, token_ids, initial, block_mask):
    rows, feats = activations.shape
    outc = initial.shape[1]
    depth = feats * n_row * n_col
    step_size = rows / (depth + 2.0 * math.sqrt(depth * rows) + rows)
    wt = weigh(activations, token_ids).T
    mask = expanded_mask(block_mask, feats, n_col)
    bf, f32 = jnp.bfloat16, jnp.float32
    small = rows // (n_row * n_col)
    dma = pltpu.SemaphoreType.DMA
    nx = n_col // 2
    any_spec = pl.BlockSpec(memory_space=pl.ANY)
    vmem_spec = pl.BlockSpec(memory_space=pltpu.VMEM)
    wt_cut = wt.reshape(PIECES, feats // PIECES, rows)
    wt_all, act_all, current = pl.pallas_call(
        functools.partial(exchange_kernel, n_row, n_col, step_size),
        out_shape=(
            jax.ShapeDtypeStruct((n_row, PIECES, feats // PIECES, rows), bf),
            jax.ShapeDtypeStruct((n_col, rows, feats), bf),
            jax.ShapeDtypeStruct((feats, outc), f32),
        ),
        in_specs=[any_spec, any_spec] + [vmem_spec] * 4,
        out_specs=(any_spec, any_spec, vmem_spec),
        scratch_shapes=[
            pltpu.VMEM((ITERS, n_col, n_row, small, outc), f32),
            pltpu.VMEM((ITERS, n_col, n_row, small, outc), f32),
            pltpu.VMEM((ITERS, n_row, small, outc), f32),
            pltpu.VMEM((ITERS, n_row, small, outc), f32),
            pltpu.VMEM((ITERS, n_col, n_row, small, outc), f32),
            pltpu.VMEM((feats, 2 * outc), bf),
            pltpu.VMEM((rows, 2 * outc), bf),
            dma((3, n_row, PIECES)), dma((n_row, PIECES)),
            dma((2 * nx,)), dma((n_col,)), dma((2,)),
            dma((ITERS, n_col)), dma((ITERS, n_col)),
            dma((ITERS, n_row)), dma((ITERS, n_row)),
            dma((ITERS, n_row)), dma((ITERS, n_row)),
            dma((ITERS, n_col)), dma((ITERS, n_col)),
        ],
        compiler_params=pltpu.CompilerParams(
            collective_id=0, has_side_effects=True, vmem_limit_bytes=VMEM_LIMIT),
    )(wt_cut, activations, wt, activations, initial, mask)

    tile = feats // PIECES
    wt_tiles = wt_all.reshape(n_row * PIECES, tile, rows)
    gram = pl.pallas_call(
        functools.partial(gram_kernel, 1.0 / rows),
        grid=(n_row * PIECES,),
        out_shape=jax.ShapeDtypeStruct((n_row, 1, feats, n_col * feats), f32),
        in_specs=[
            pl.BlockSpec((1, tile, rows), lambda i: (i, 0, 0)),
            pl.BlockSpec((n_col, rows, feats), lambda i: (0, 0, 0)),
        ],
        out_specs=pl.BlockSpec((1, 1, tile, n_col * feats), lambda i: (i // PIECES, 0, i % PIECES, 0)),
        compiler_params=pltpu.CompilerParams(vmem_limit_bytes=VMEM_LIMIT),
    )(wt_tiles, act_all)
    return gram, current


def shards(n_row, n_col, activations, token_ids, initial, block_mask):
    rows, feats = activations.shape
    if feats % (BLOCK * PIECES) == 0 and n_row % 2 == 0 and n_col % 2 == 0 and rows % (8 * n_row * n_col) == 0:
        return kernel_shards(n_row, n_col, activations, token_ids, initial, block_mask)
    weighted = weigh(activations, token_ids)
    column_panel = lax.all_gather(activations, "col", axis=1, tiled=True)
    gram_tile = lax.dot_general(
        lax.all_gather(weighted, "row", axis=1, tiled=True),
        column_panel,
        (((0,), (0,)), ((), ())),
        preferred_element_type=jnp.float32,
    ) * (1.0 / rows)
    mask_full = expanded_mask(block_mask, feats, n_col)
    depth = feats * n_row * n_col
    step_size = rows / (depth + 2.0 * math.sqrt(depth * rows) + rows)
    current = mask_full * initial
    for iteration in range(ITERS):
        change_now = current - initial
        projected = jnp.dot(
            activations.astype(jnp.float32), change_now, precision=lax.Precision.HIGHEST
        )
        totals = lax.psum(projected, ("row", "col"))
        pulled = lax.dot_general(
            weighted.astype(jnp.float32),
            totals,
            (((0,), (0,)), ((), ())),
            precision=lax.Precision.HIGHEST,
        ) * (1.0 / rows)
        current = mask_full * (current - step_size * pulled)
    return gram_tile.reshape(n_row, 1, feats, gram_tile.shape[1]), current


def solution(mesh):
    in_specs = (
        P("groups", ("row", "col")),
        P("groups"),
        P(("groups", "row", "col"), None),
        P("groups", None),
    )
    out_specs = (P("groups", "col", None, "row"), P(("groups", "row", "col"), None))
    body = functools.partial(shards, mesh.shape["row"], mesh.shape["col"])
    return jax.shard_map(body, mesh=mesh, in_specs=in_specs, out_specs=out_specs, check_vma=False)
```

time: 426 us -> 161 us (0.38)
  waiting for transfers between devices: 366 us -> 0 us
  Pallas kernels: 0 us -> 152 us
  matrix products: 41.3 us -> 1.11 us
  between operations: 15.6 us -> 0.74 us
  local copies, waits for them, and re-layouts: 0.62 us -> 5.11 us
    psum x2 -> x0, waiting for transfers between devices: 365 us -> none  [shards(): totals = lax.psum(projected, ('row', 'col'))]
    pallas_call x0 -> x2, Pallas kernels: none -> 152 us  [the longest x1 128 us: kernel_shards(): pl.pallas_call(functools.partial(exchange_kernel, n_row, n_col, step_size...]
    dot_general x6 -> x1, matrix products: 41.3 us -> 1.11 us  [expanded_mask(): jnp.dot(selector, block_mask.astype(jnp.float32), precision=lax.Precision...]
    unnamed x6 -> x9, local copies, waits for them, and re-layouts: 0.02 us -> 4.51 us
  transfers between devices with their start and end apart: 4 -> 0, of which waited for: 2 -> 0; matrix products, arithmetic and copies ran while one was open for 1% -> 0% of each run, Pallas kernels for 0% -> 0%
where the time goes in v1:
time: 161 us
  Pallas kernels  152 us (94%)
  local copies, waits for them, and re-layouts  5.11 us (3%)
  other arithmetic  1.8 us (1%)
    pallas_call x1, Pallas kernels, kernel_shards(): pl.pallas_call(functools.partial(exchange_kernel, n_row, n_col, step_size...  128 us
    pallas_call x1, Pallas kernels, kernel_shards(): pl.pallas_call(functools.partial(gram_kernel, 1.0 / rows), grid=(n_row *...  24.1 us
    unnamed x9, local copies, waits for them, and re-layouts  4.51 us

profile of v1, /device:TPU:1, one launch (start us, length us, event | category | flops | bytes accessed | tf_op | source)
XLA Modules:
  0.0 160.6 jit_solution(395608785526132391)
XLA Ops:
  0.7 1.3 convert_reduce_fusion
  2.0 0.0 copy-start
  2.0 0.0 copy-start.2
  2.0 1.1 fusion
  3.1 0.6 broadcast_in_dim.2
  3.8 1.5 copy.8
  5.3 0.2 fusion.6.wt
  5.5 0.2 multiply_convert_fusion
  5.8 0.0 copy-done
  5.8 0.0 copy-done.2
  5.8 127.7 %shard_map.59 = (bf16[8,2,256,1024]{3,2,1,0:T(8,128)(2,1)}, bf16[4,1024,512]{2,1,0:T(8,128)(2,1)}, f32[512,256]{1,0:T(8,128)S(1)}) custom-call(bf16[2,256,1024]{2,1,0:T(8,128)(2,1)S(1)} %bitcast.9, bf16[1024,512]{1,0:T(8,128)(2,1)S(1)} %copy-done, bf16[512,1024]{1,0:T(8,128)(2,1)S(1)} %fusion.6.wt, bf16[1024,512]{1,0:T(8,128)(2,1)S(1)} %copy-done, ...), custom_call_target="tpu_custom_call" | custom-call | tf_op jit(solution)/shard_map/pallas_call | solution.py:257
  133.5 0.0 copy-start.1
  133.5 2.2 %copy-done.1 = bf16[4,1024,512]{2,1,0:T(8,128)(2,1)S(1)} copy-done((bf16[4,1024,512]{2,1,0:T(8,128)(2,1)S(1)}, bf16[4,1024,512]{2,1,0:T(8,128)(2,1)}, u32[]{:S(2)}) %copy-start.1) | copy-done | bytes 4194328
  135.7 24.1 %shard_map.60 = f32[8,1,512,2048]{3,2,1,0:T(8,128)} custom-call(bf16[16,256,1024]{2,1,0:T(8,128)(2,1)} %bitcast.11, bf16[4,1024,512]{2,1,0:T(8,128)(2,1)S(1)} %copy-done.1), custom_call_target="tpu_custom_call" | custom-call | tf_op jit(solution)/shard_map/pallas_call | solution.py:287
  159.8 0.8 copy.15
  (3 shorter events, 0.1 us)
Async XLA Ops:
  2.0 3.8 %copy-start = (bf16[1024,512]{1,0:T(8,128)(2,1)S(1)}, bf16[1024,512]{1,0:T(8,128)(2,1)}, u32[]{:S(2)}) copy-start(bf16[1024,512]{1,0:T(8,128)(2,1)} %act.1) | copy-start | bytes 3145732
  2.0 3.8 %copy-start.2 = (f32[512,256]{1,0:T(8,128)S(1)}, f32[512,256]{1,0:T(8,128)}, u32[]{:S(2)}) copy-start(f32[512,256]{1,0:T(8,128)} %init.1) | copy-start | bytes 1572868
  133.5 2.2 %copy-start.1 = (bf16[4,1024,512]{2,1,0:T(8,128)(2,1)S(1)}, bf16[4,1024,512]{2,1,0:T(8,128)(2,1)}, u32[]{:S(2)}) copy-start(bf16[4,1024,512]{2,1,0:T(8,128)(2,1)} %get-tuple-element.6.act) | copy-start | bytes 12582916

commit v2 on v1

--- a/solution.py
+++ b/solution.py
@@ -168,8 +168,7 @@
         tot[it, c, r] = acc
         exchange([send(tot.at[it, c, r], tot.at[it, c, r], s3.at[it, k], r3.at[it, r], {"row": p})
                   for k, p in enumerate(row_peers)])
-        if it > 0:
-            next_hop()
+        next_hop()
         for k, p in enumerate(row_peers):
             send(tot.at[it, c, p], tot.at[it, c, p], s3.at[it, k], r3.at[it, p], {"row": p}).wait_recv()
         exchange([send(tot.at[it, c], tot.at[it, c], s4.at[it, k], r4.at[it, c], {"col": p})

time: 161 us -> 162 us (level)
  no operation moved by 1% of the time
where the time goes in v2:
time: 162 us; the launch traced here: 161 us
  Pallas kernels  152 us (94%)
  local copies, waits for them, and re-layouts  5.11 us (3%)
  other arithmetic  1.8 us (1%)
    pallas_call x1, Pallas kernels, kernel_shards(): pl.pallas_call(functools.partial(exchange_kernel, n_row, n_col, step_size...  128 us
    pallas_call x1, Pallas kernels, kernel_shards(): pl.pallas_call(functools.partial(gram_kernel, 1.0 / rows), grid=(n_row *...  24.1 us
    unnamed x9, local copies, waits for them, and re-layouts  4.51 us

profile of v2, /device:TPU:1, one launch (start us, length us, event | category | flops | bytes accessed | tf_op | source)
XLA Modules:
  0.0 161.1 jit_solution(9684163810339521165)
XLA Ops:
  0.7 1.3 convert_reduce_fusion
  2.0 0.0 copy-start
  2.0 0.0 copy-start.2
  2.0 1.1 fusion
  3.1 0.6 broadcast_in_dim.2
  3.8 1.5 copy.8
  5.3 0.2 fusion.6.wt
  5.5 0.2 multiply_convert_fusion
  5.8 0.0 copy-done
  5.8 0.0 copy-done.2
  5.8 128.3 %shard_map.59 = (bf16[8,2,256,1024]{3,2,1,0:T(8,128)(2,1)}, bf16[4,1024,512]{2,1,0:T(8,128)(2,1)}, f32[512,256]{1,0:T(8,128)S(1)}) custom-call(bf16[2,256,1024]{2,1,0:T(8,128)(2,1)S(1)} %bitcast.9, bf16[1024,512]{1,0:T(8,128)(2,1)S(1)} %copy-done, bf16[512,1024]{1,0:T(8,128)(2,1)S(1)} %fusion.6.wt, bf16[1024,512]{1,0:T(8,128)(2,1)S(1)} %copy-done, ...), custom_call_target="tpu_custom_call" | custom-call | tf_op jit(solution)/shard_map/pallas_call | solution.py:256
  134.0 0.0 copy-start.1
  134.1 2.2 %copy-done.1 = bf16[4,1024,512]{2,1,0:T(8,128)(2,1)S(1)} copy-done((bf16[4,1024,512]{2,1,0:T(8,128)(2,1)S(1)}, bf16[4,1024,512]{2,1,0:T(8,128)(2,1)}, u32[]{:S(2)}) %copy-start.1) | copy-done | bytes 4194328
  136.2 24.1 %shard_map.60 = f32[8,1,512,2048]{3,2,1,0:T(8,128)} custom-call(bf16[16,256,1024]{2,1,0:T(8,128)(2,1)} %bitcast.11, bf16[4,1024,512]{2,1,0:T(8,128)(2,1)S(1)} %copy-done.1), custom_call_target="tpu_custom_call" | custom-call | tf_op jit(solution)/shard_map/pallas_call | solution.py:286
  160.3 0.8 copy.15
  (3 shorter events, 0.1 us)
Async XLA Ops:
  2.0 3.8 %copy-start = (bf16[1024,512]{1,0:T(8,128)(2,1)S(1)}, bf16[1024,512]{1,0:T(8,128)(2,1)}, u32[]{:S(2)}) copy-start(bf16[1024,512]{1,0:T(8,128)(2,1)} %act.1) | copy-start | bytes 3145732
  2.0 3.8 %copy-start.2 = (f32[512,256]{1,0:T(8,128)S(1)}, f32[512,256]{1,0:T(8,128)}, u32[]{:S(2)}) copy-start(f32[512,256]{1,0:T(8,128)} %init.1) | copy-start | bytes 1572868
  134.0 2.2 %copy-start.1 = (bf16[4,1024,512]{2,1,0:T(8,128)(2,1)S(1)}, bf16[4,1024,512]{2,1,0:T(8,128)(2,1)}, u32[]{:S(2)}) copy-start(bf16[4,1024,512]{2,1,0:T(8,128)(2,1)} %get-tuple-element.6.act) | copy-start | bytes 12582916

commit v3 on v1

--- a/solution.py
+++ b/solution.py
@@ -11,6 +11,7 @@
 BLOCK = 128
 ITERS = 2
 PIECES = 2
+TILES = 1
 VMEM_LIMIT = 48 * 1024 * 1024
 
 
@@ -282,17 +283,17 @@
             collective_id=0, has_side_effects=True, vmem_limit_bytes=VMEM_LIMIT),
     )(wt_cut, activations, wt, activations, initial, mask)
 
-    tile = feats // PIECES
-    wt_tiles = wt_all.reshape(n_row * PIECES, tile, rows)
+    tile = feats // TILES
+    wt_tiles = wt_all.reshape(n_row * TILES, tile, rows)
     gram = pl.pallas_call(
         functools.partial(gram_kernel, 1.0 / rows),
-        grid=(n_row * PIECES,),
+        grid=(n_row * TILES,),
         out_shape=jax.ShapeDtypeStruct((n_row, 1, feats, n_col * feats), f32),
         in_specs=[
             pl.BlockSpec((1, tile, rows), lambda i: (i, 0, 0)),
             pl.BlockSpec((n_col, rows, feats), lambda i: (0, 0, 0)),
         ],
-        out_specs=pl.BlockSpec((1, 1, tile, n_col * feats), lambda i: (i // PIECES, 0, i % PIECES, 0)),
+        out_specs=pl.BlockSpec((1, 1, tile, n_col * feats), lambda i: (i // TILES, 0, i % TILES, 0)),
         compiler_params=pltpu.CompilerParams(vmem_limit_bytes=VMEM_LIMIT),
     )(wt_tiles, act_all)
     return gram, current

time: 161 us -> 159 us (0.988)
  Pallas kernels: 152 us -> 150 us
    pallas_call x1, Pallas kernels: 24.1 us -> 22 us  [kernel_shards(): pl.pallas_call(functools.partial(gram_kernel, 1.0 / rows), grid=(n_row *...]
where the time goes in v3:
time: 159 us
  Pallas kernels  150 us (94%)
  local copies, waits for them, and re-layouts  5.11 us (3%)
  other arithmetic  1.8 us (1%)
    pallas_call x1, Pallas kernels, kernel_shards(): pl.pallas_call(functools.partial(exchange_kernel, n_row, n_col, step_size...  128 us
    pallas_call x1, Pallas kernels, kernel_shards(): pl.pallas_call(functools.partial(gram_kernel, 1.0 / rows), grid=(n_row *...  22 us
    unnamed x9, local copies, waits for them, and re-layouts  4.51 us

profile of v3, /device:TPU:1, one launch (start us, length us, event | category | flops | bytes accessed | tf_op | source)
XLA Modules:
  0.0 158.5 jit_solution(15877252771095124366)
XLA Ops:
  0.7 1.3 convert_reduce_fusion
  2.0 0.0 copy-start
  2.0 0.0 copy-start.2
  2.0 1.1 fusion
  3.1 0.6 broadcast_in_dim.2
  3.8 1.5 copy.8
  5.3 0.2 fusion.6.wt
  5.5 0.2 multiply_convert_fusion
  5.8 0.0 copy-done
  5.8 0.0 copy-done.2
  5.8 127.7 %shard_map.59 = (bf16[8,2,256,1024]{3,2,1,0:T(8,128)(2,1)}, bf16[4,1024,512]{2,1,0:T(8,128)(2,1)}, f32[512,256]{1,0:T(8,128)S(1)}) custom-call(bf16[2,256,1024]{2,1,0:T(8,128)(2,1)S(1)} %bitcast.9, bf16[1024,512]{1,0:T(8,128)(2,1)S(1)} %copy-done, bf16[512,1024]{1,0:T(8,128)(2,1)S(1)} %fusion.6.wt, bf16[1024,512]{1,0:T(8,128)(2,1)S(1)} %copy-done, ...), custom_call_target="tpu_custom_call" | custom-call | tf_op jit(solution)/shard_map/pallas_call | solution.py:258
  133.5 0.0 copy-start.1
  133.5 2.2 %copy-done.1 = bf16[4,1024,512]{2,1,0:T(8,128)(2,1)S(1)} copy-done((bf16[4,1024,512]{2,1,0:T(8,128)(2,1)S(1)}, bf16[4,1024,512]{2,1,0:T(8,128)(2,1)}, u32[]{:S(2)}) %copy-start.1) | copy-done | bytes 4194328
  135.7 22.0 %shard_map.60 = f32[8,1,512,2048]{3,2,1,0:T(8,128)} custom-call(bf16[8,512,1024]{2,1,0:T(8,128)(2,1)} %bitcast.11, bf16[4,1024,512]{2,1,0:T(8,128)(2,1)S(1)} %copy-done.1), custom_call_target="tpu_custom_call" | custom-call | tf_op jit(solution)/shard_map/pallas_call | solution.py:288
  157.7 0.8 copy.15
  (3 shorter events, 0.1 us)
Async XLA Ops:
  2.0 3.8 %copy-start = (bf16[1024,512]{1,0:T(8,128)(2,1)S(1)}, bf16[1024,512]{1,0:T(8,128)(2,1)}, u32[]{:S(2)}) copy-start(bf16[1024,512]{1,0:T(8,128)(2,1)} %act.1) | copy-start | bytes 3145732
  2.0 3.8 %copy-start.2 = (f32[512,256]{1,0:T(8,128)S(1)}, f32[512,256]{1,0:T(8,128)}, u32[]{:S(2)}) copy-start(f32[512,256]{1,0:T(8,128)} %init.1) | copy-start | bytes 1572868
  133.5 2.2 %copy-start.1 = (bf16[4,1024,512]{2,1,0:T(8,128)(2,1)S(1)}, bf16[4,1024,512]{2,1,0:T(8,128)(2,1)}, u32[]{:S(2)}) copy-start(bf16[4,1024,512]{2,1,0:T(8,128)(2,1)} %get-tuple-element.6.act) | copy-start | bytes 12582916
